TPU v7x, 32 devices: a whole 2x2x4 slice. The times are simulated.
32 devices in a mesh: dp: 16 (over z, y, core), tensor: 2 (over x).
Axes of the slice: x: 2, y: 2, z: 4, core: 2. Of those that a mesh axis runs over, the one named last changes fastest.
Arguments:
- visual: bfloat16 [6912, 768], P(('dp', 'tensor')), may hold values from -6 to 6
- query: bfloat16 [8192, 768], P(('dp', 'tensor')), may hold values from -6 to 6
- seg_ids: int32 [16, 512], P('dp'), may hold values from 0 to 31, as said below
- shifts: int32 [16, 2], P('dp'), may hold values from 0 to 11
- valid_rows: int32 [16], P('dp'), may hold values from 19 to 36
- attn_in: float32 [4, 768, 3, 768], P(None, 'dp', None, 'tensor'), may hold values from -0.21875 to 0.21875
- attn_out: float32 [4, 768, 768], P(None, 'tensor', 'dp'), may hold values from -1.25 to 1.25
- mlp_in: float32 [2, 768, 3072], P(None, 'dp', 'tensor'), may hold values from -0.21875 to 0.21875
- mlp_out: float32 [2, 3072, 768], P(None, 'tensor', 'dp'), may hold values from -0.109375 to 0.109375
- gains: float32 [6, 768], P(None, 'dp'), may hold values from 0.5 to 1.5
- cot_visual: bfloat16 [6912, 768], P(('dp', 'tensor')), may hold values from -6 to 6
- cot_query: bfloat16 [8192, 768], P(('dp', 'tensor')), may hold values from -6 to 6
Outputs:
- out_visual: bfloat16 [6912, 768], P(('dp', 'tensor'))
- out_query: bfloat16 [8192, 768], P(('dp', 'tensor'))
- grad_visual: bfloat16 [6912, 768], P(('dp', 'tensor'))
- grad_query: bfloat16 [8192, 768], P(('dp', 'tensor'))
- grad_attn_in: float32 [4, 768, 3, 768], P(None, 'dp', None, 'tensor')
- grad_attn_out: float32 [4, 768, 768], P(None, 'tensor', 'dp')
- grad_mlp_in: float32 [2, 768, 3072], P(None, 'dp', 'tensor')
- grad_mlp_out: float32 [2, 3072, 768], P(None, 'tensor', 'dp')
- grad_gains: float32 [6, 768], P(None, 'dp')
Inputs may be any that keep to these rules, and one draw needn't show every extreme that they name: `seg_ids`: in each page the ids start at 0, rise by at most one from a slot to the next and never fall, and the last slot holds id 512 // 16 - 1; slots 512 // 2 - 512 // 8 to 320 share one id.
All inputs are finite; a program needn't handle non-finite values.
Results may differ from a plain program's by a relative error of at most 0.025.
Values may be sent and summed in bfloat16 or wider, within the bound.
No kernel may reach another device: no remote copies, remote signals or barrier semaphores. Data moves between devices by JAX's collectives and lax.ppermute only.
A program may use at most 192 MiB of HBM per device.

v0:
```python
import jax
import jax.numpy as jnp
from jax import lax
from jax.sharding import PartitionSpec as P

HD = 64
WIN = 12
PH = 36
PW = 12


EPSILON = 1e-05
MASKED = -1e30
ROOT_HALF = 0.7071067811865476
INV_ROOT_TAU = 0.3989422804014327


def tile_grid(page_grid):
    tiled = page_grid.reshape(PH // WIN, WIN, PW // WIN, WIN, -1).transpose(0, 2, 1, 3, 4)
    return tiled.reshape(PH // WIN * (PW // WIN), WIN * WIN, -1)


def untile_grid(blocks):
    page_grid = blocks.reshape(PH // WIN, PW // WIN, WIN, WIN, -1).transpose(0, 2, 1, 3, 4)
    return page_grid.reshape(PH, PW, -1)


def to_windows(row_block, offset):
    page_grid = jnp.roll(row_block.reshape(PH, PW, -1), (-offset[0], -offset[1]), axis=(0, 1))
    return tile_grid(page_grid)


def from_windows(blocks, offset):
    page_grid = jnp.roll(untile_grid(blocks), (offset[0], offset[1]), axis=(0, 1))
    return page_grid.reshape(PH * PW, -1)


def window_mask(offset, rows_valid):
    row_place = jnp.arange(PH, dtype=jnp.int32) + offset[0]
    col_place = jnp.arange(PW, dtype=jnp.int32) + offset[1]
    region = (row_place >= PH).astype(jnp.int32)[:, None] * 2 + (col_place >= PW).astype(jnp.int32)[
        None, :
    ]
    usable_rows = jnp.broadcast_to((row_place % PH < rows_valid)[:, None], (PH, PW)).astype(
        jnp.int32
    )
    regions = tile_grid(region[:, :, None])[:, :, 0]
    usable = tile_grid(usable_rows[:, :, None])[:, :, 0] > 0
    same_region = regions[:, :, None] == regions[:, None, :]
    itself = jnp.eye(WIN * WIN, dtype=bool)[None]
    return same_region & (usable[:, None, :] | itself)


def normalize(row_block, gain_row):
    average = jnp.mean(row_block, axis=-1, keepdims=True)
    centred = row_block - average
    inverse = lax.rsqrt(jnp.mean(centred * centred, axis=-1, keepdims=True) + EPSILON)
    unit_rows = centred * inverse
    return ((unit_rows * gain_row.astype(jnp.float32)).astype(jnp.bfloat16), unit_rows, inverse)


def normalize_back(grad_rows, unit_rows, inverse, gain_row):
    scaled = grad_rows * gain_row.astype(jnp.float32)
    centre = jnp.mean(scaled, axis=-1, keepdims=True)
    slope_mean = jnp.mean(scaled * unit_rows, axis=-1, keepdims=True)
    return (
        inverse * (scaled - centre - unit_rows * slope_mean),
        jnp.sum(grad_rows * unit_rows, axis=0),
    )


def gelu_slope(hidden):
    return (
        0.5 * (1.0 + lax.erf(hidden * ROOT_HALF))
        + hidden * jnp.exp(-0.5 * hidden * hidden) * INV_ROOT_TAU
    )


def heads_first(block, slot_count, head_width):
    block_count, length = (block.shape[0], block.shape[1])
    shaped = block.reshape(block_count, length, slot_count, -1, head_width).transpose(2, 3, 0, 1, 4)
    return tuple((shaped[position] for position in range(slot_count)))


def heads_last(head_parts):
    stacked = jnp.stack(head_parts)
    slot_count, head_count, block_count, length, head_width = stacked.shape
    return stacked.transpose(2, 3, 0, 1, 4).reshape(
        block_count, length, slot_count * head_count * head_width
    )


def attend_forward(queries, keys, values, allowed, logit_scale):

    def one_head(head_parts):
        per_head_queries, per_head_keys, per_head_values = head_parts
        attention_logits = (
            jnp.einsum(
                "jty,joy->jto", per_head_queries, per_head_keys, preferred_element_type=jnp.float32
            )
            * logit_scale
        )
        attention_logits = jnp.where(allowed, attention_logits, MASKED)
        highest = jnp.max(attention_logits, axis=-1, keepdims=True)
        weights = jnp.exp(attention_logits - highest)
        totals = jnp.sum(weights, axis=-1, keepdims=True)
        attention_probs = (weights / totals).astype(jnp.bfloat16)
        blended_rows = jnp.einsum(
            "osy,oya->osa", attention_probs, per_head_values, preferred_element_type=jnp.float32
        )
        return (blended_rows.astype(jnp.bfloat16), highest + jnp.log(totals))

    return lax.map(one_head, (queries, keys, values))


def attend_backward(queries, keys, values, allowed, logit_scale, grad_heads, log_totals):

    def one_head(head_parts):
        per_head_queries, per_head_keys, per_head_values, per_head_gradient, head_log = head_parts
        attention_logits = (
            jnp.einsum(
                "jty,joy->jto", per_head_queries, per_head_keys, preferred_element_type=jnp.float32
            )
            * logit_scale
        )
        attention_logits = jnp.where(allowed, attention_logits, MASKED)
        attention_probs = jnp.exp(attention_logits - head_log)
        grad_chances = jnp.einsum(
            "jty,joy->jto", per_head_gradient, per_head_values, preferred_element_type=jnp.float32
        )
        grad_values = jnp.einsum(
            "rfc,rfh->rch",
            attention_probs.astype(jnp.bfloat16),
            per_head_gradient,
            preferred_element_type=jnp.float32,
        )
        centre = jnp.sum(grad_chances * attention_probs, axis=-1, keepdims=True)
        score_gradient = (attention_probs * (grad_chances - centre)).astype(jnp.bfloat16)
        grad_queries = (
            jnp.einsum(
                "osy,oya->osa", score_gradient, per_head_keys, preferred_element_type=jnp.float32
            )
            * logit_scale
        )
        grad_keys = (
            jnp.einsum(
                "rfc,rfh->rch", score_gradient, per_head_queries, preferred_element_type=jnp.float32
            )
            * logit_scale
        )
        return (
            grad_queries.astype(jnp.bfloat16),
            grad_keys.astype(jnp.bfloat16),
            grad_values.astype(jnp.bfloat16),
        )

    return lax.map(one_head, (queries, keys, values, grad_heads, log_totals))


def project(row_block, weight_slot):
    flat_weight = weight_slot.reshape(weight_slot.shape[0], -1)
    return jnp.dot(row_block, flat_weight, preferred_element_type=jnp.float32).astype(jnp.bfloat16)


def project_back(row_block, grad_rows, weight_slot):
    flat_weight = weight_slot.reshape(weight_slot.shape[0], -1)
    grad_input = jnp.einsum("rc,dc->rd", grad_rows, flat_weight, preferred_element_type=jnp.float32)
    grad_weight = jnp.einsum("rd,rc->dc", row_block, grad_rows, preferred_element_type=jnp.float32)
    return (grad_input, grad_weight.reshape(weight_slot.shape))


def output_back(blended_rows, grad_rows, weight_out):
    grad_mixed = jnp.einsum(
        "rd,hd->rh", grad_rows, weight_out, preferred_element_type=jnp.float32
    ).astype(jnp.bfloat16)
    grad_weight = jnp.einsum(
        "rh,rd->hd", blended_rows, grad_rows, preferred_element_type=jnp.float32
    )
    return (grad_mixed, grad_weight)


def window_forward(row_block, weight_in, allowed, logit_scale, head_width, offset):
    window_rows = to_windows(project(row_block, weight_in), offset)
    per_head_queries, per_head_keys, per_head_values = heads_first(window_rows, 3, head_width)
    blended_rows, log_totals = attend_forward(
        per_head_queries, per_head_keys, per_head_values, allowed, logit_scale
    )
    return (
        (per_head_queries, per_head_keys, per_head_values, log_totals),
        from_windows(heads_last((blended_rows,)), offset),
    )


def window_backward(
    row_block, weight_in, allowed, logit_scale, head_width, offset, kept, grad_mixed
):
    per_head_queries, per_head_keys, per_head_values, log_totals = kept
    (grad_heads,) = heads_first(to_windows(grad_mixed, offset), 1, head_width)
    grad_q, grad_k, grad_v = attend_backward(
        per_head_queries,
        per_head_keys,
        per_head_values,
        allowed,
        logit_scale,
        grad_heads,
        log_totals,
    )
    flat_grads = from_windows(heads_last((grad_q, grad_k, grad_v)), offset)
    return project_back(row_block, flat_grads, weight_in)


def cross_forward(query_rows, source_rows, weight_in, allowed, logit_scale, head_width):
    query_proj = project(query_rows, weight_in[:, 0:1])
    source_proj = project(source_rows, weight_in[:, 1:3])
    (per_head_queries,) = heads_first(query_proj[None], 1, head_width)
    per_head_keys, per_head_values = heads_first(source_proj[None], 2, head_width)
    blended_rows, log_totals = attend_forward(
        per_head_queries, per_head_keys, per_head_values, allowed, logit_scale
    )
    return (
        (per_head_queries, per_head_keys, per_head_values, log_totals),
        heads_last((blended_rows,))[0],
    )


def cross_backward(
    query_rows, source_rows, weight_in, allowed, logit_scale, head_width, kept, grad_mixed
):
    per_head_queries, per_head_keys, per_head_values, log_totals = kept
    (grad_heads,) = heads_first(grad_mixed[None], 1, head_width)
    grad_q, grad_k, grad_v = attend_backward(
        per_head_queries,
        per_head_keys,
        per_head_values,
        allowed,
        logit_scale,
        grad_heads,
        log_totals,
    )
    query_grad, query_weight = project_back(query_rows, heads_last((grad_q,))[0], weight_in[:, 0:1])
    source_grad, source_weight = project_back(
        source_rows, heads_last((grad_k, grad_v))[0], weight_in[:, 1:3]
    )
    return (query_grad, source_grad, jnp.concatenate([query_weight, source_weight], axis=1))


def mlp_forward(row_block, weight_up, weight_down):
    hidden = jnp.dot(row_block, weight_up, preferred_element_type=jnp.float32)
    active = jax.nn.gelu(hidden, approximate=False).astype(jnp.bfloat16)
    return (hidden, active, jnp.dot(active, weight_down, preferred_element_type=jnp.float32))


def mlp_backward(row_block, hidden, active, grad_rows, weight_up, weight_down):
    grad_active = jnp.einsum(
        "rd,fd->rf", grad_rows, weight_down, preferred_element_type=jnp.float32
    )
    grad_hidden = (grad_active * gelu_slope(hidden)).astype(jnp.bfloat16)
    grad_input = jnp.einsum("rf,df->rd", grad_hidden, weight_up, preferred_element_type=jnp.float32)
    grad_up = jnp.einsum("rd,rf->df", row_block, grad_hidden, preferred_element_type=jnp.float32)
    grad_down = jnp.einsum("rf,rd->fd", active, grad_rows, preferred_element_type=jnp.float32)
    return (grad_input, grad_up, grad_down)


def spread_rows(first_rows, second_rows):
    return (
        lax.all_gather(first_rows, "tensor", axis=0, tiled=True),
        lax.all_gather(second_rows, "tensor", axis=0, tiled=True),
    )


def settle_rows(first_part, second_part):
    return (
        lax.psum_scatter(
            first_part.astype(jnp.bfloat16), "tensor", scatter_dimension=0, tiled=True
        ).astype(jnp.float32),
        lax.psum_scatter(
            second_part.astype(jnp.bfloat16), "tensor", scatter_dimension=0, tiled=True
        ).astype(jnp.float32),
    )


def spread_grads(first_grad, second_grad):
    return (
        lax.all_gather(first_grad.astype(jnp.bfloat16), "tensor", axis=0, tiled=True),
        lax.all_gather(second_grad.astype(jnp.bfloat16), "tensor", axis=0, tiled=True),
    )


def settle_grads(first_part, second_part):
    return (
        lax.psum_scatter(
            first_part.astype(jnp.bfloat16), "tensor", scatter_dimension=0, tiled=True
        ).astype(jnp.float32),
        lax.psum_scatter(
            second_part.astype(jnp.bfloat16), "tensor", scatter_dimension=0, tiled=True
        ).astype(jnp.float32),
    )


def on_device(
    visual,
    query,
    seg_ids,
    shifts,
    valid_rows,
    attn_in,
    attn_out,
    mlp_in,
    mlp_out,
    gains,
    cot_visual,
    cot_query,
):
    logit_scale = HD ** (-0.5)
    offset = shifts[0]
    rows_valid = valid_rows[0]
    segment = seg_ids[0]
    master_in = attn_in.astype(jnp.bfloat16)
    master_out = attn_out.astype(jnp.bfloat16)
    master_up = mlp_in.astype(jnp.bfloat16)
    master_down = mlp_out.astype(jnp.bfloat16)
    master_gain = gains.astype(jnp.bfloat16)
    weight_in, weight_out, mlp_up, mlp_down, gain_rows = (
        lax.all_gather(master_in, "dp", axis=1, tiled=True),
        lax.all_gather(master_out, "dp", axis=2, tiled=True),
        lax.all_gather(master_up, "dp", axis=1, tiled=True),
        lax.all_gather(master_down, "dp", axis=2, tiled=True),
        lax.all_gather(master_gain, "dp", axis=1, tiled=True),
    )
    win_allowed = window_mask(offset, rows_valid)
    self_allowed = (segment[:, None] == segment[None, :])[None]
    patch_rows = jnp.arange(PH * PW, dtype=jnp.int32) // PW
    read_allowed = (patch_rows < rows_valid)[None, None, :]
    open_allowed = jnp.ones((1, 1, 1), dtype=bool)
    visual_in = visual.astype(jnp.float32)
    query_in = query.astype(jnp.float32)
    norm_win, unit_win, inv_win = normalize(visual_in, gain_rows[0])
    norm_self, unit_self, inv_self = normalize(query_in, gain_rows[1])
    full_win, full_self = spread_rows(norm_win, norm_self)
    kept_win, mixed_win = window_forward(
        full_win, weight_in[0], win_allowed, logit_scale, HD, offset
    )
    kept_self, mixed_self = cross_forward(
        full_self, full_self, weight_in[1], self_allowed, logit_scale, HD
    )
    add_win, add_self = settle_rows(
        jnp.dot(mixed_win, weight_out[0], preferred_element_type=jnp.float32),
        jnp.dot(mixed_self, weight_out[1], preferred_element_type=jnp.float32),
    )
    visual_one = visual_in + add_win
    query_one = query_in + add_self
    norm_vis, unit_vis, inv_vis = normalize(visual_one, gain_rows[2])
    norm_qry, unit_qry, inv_qry = normalize(query_one, gain_rows[3])
    full_vis, full_qry = spread_rows(norm_vis, norm_qry)
    kept_read, mixed_read = cross_forward(
        full_qry, full_vis, weight_in[2], read_allowed, logit_scale, HD
    )
    kept_look, mixed_look = cross_forward(
        full_vis, full_qry, weight_in[3], open_allowed, logit_scale, HD
    )
    add_look, add_read = settle_rows(
        jnp.dot(mixed_look, weight_out[3], preferred_element_type=jnp.float32),
        jnp.dot(mixed_read, weight_out[2], preferred_element_type=jnp.float32),
    )
    visual_two = visual_one + add_look
    query_two = query_one + add_read
    norm_mv, unit_mv, inv_mv = normalize(visual_two, gain_rows[4])
    norm_mq, unit_mq, inv_mq = normalize(query_two, gain_rows[5])
    full_mv, full_mq = spread_rows(norm_mv, norm_mq)
    hidden_vis, active_vis, part_vis = mlp_forward(full_mv, mlp_up[0], mlp_down[0])
    hidden_qry, active_qry, part_qry = mlp_forward(full_mq, mlp_up[1], mlp_down[1])
    add_mv, add_mq = settle_rows(part_vis, part_qry)
    visual_out = visual_two + add_mv
    query_out = query_two + add_mq
    weight_in, weight_out, mlp_up, mlp_down, gain_rows = (
        lax.all_gather(master_in, "dp", axis=1, tiled=True),
        lax.all_gather(master_out, "dp", axis=2, tiled=True),
        lax.all_gather(master_up, "dp", axis=1, tiled=True),
        lax.all_gather(master_down, "dp", axis=2, tiled=True),
        lax.all_gather(master_gain, "dp", axis=1, tiled=True),
    )
    grad_visual = cot_visual.astype(jnp.float32)
    grad_query = cot_query.astype(jnp.float32)
    down_mv, down_mq = spread_grads(grad_visual, grad_query)
    rows_mv, up_vis, down_vis = mlp_backward(
        full_mv, hidden_vis, active_vis, down_mv, mlp_up[0], mlp_down[0]
    )
    rows_mq, up_qry, down_qry = mlp_backward(
        full_mq, hidden_qry, active_qry, down_mq, mlp_up[1], mlp_down[1]
    )
    grad_up = jnp.stack([up_vis, up_qry])
    grad_down = jnp.stack([down_vis, down_qry])
    settle_mv, settle_mq = settle_grads(rows_mv, rows_mq)
    extra_vis, gain_four = normalize_back(settle_mv, unit_mv, inv_mv, gain_rows[4])
    extra_qry, gain_five = normalize_back(settle_mq, unit_mq, inv_mq, gain_rows[5])
    grad_visual = grad_visual + extra_vis
    grad_query = grad_query + extra_qry
    down_look, down_read = spread_grads(grad_visual, grad_query)
    mixed_grad_read, out_two = output_back(mixed_read, down_read, weight_out[2])
    mixed_grad_look, out_three = output_back(mixed_look, down_look, weight_out[3])
    query_two_grad, visual_two_grad, in_two = cross_backward(
        full_qry, full_vis, weight_in[2], read_allowed, logit_scale, HD, kept_read, mixed_grad_read
    )
    visual_three_grad, query_three_grad, in_three = cross_backward(
        full_vis, full_qry, weight_in[3], open_allowed, logit_scale, HD, kept_look, mixed_grad_look
    )
    settle_vis, settle_qry = settle_grads(
        visual_two_grad + visual_three_grad, query_two_grad + query_three_grad
    )
    extra_vis, gain_two = normalize_back(settle_vis, unit_vis, inv_vis, gain_rows[2])
    extra_qry, gain_three = normalize_back(settle_qry, unit_qry, inv_qry, gain_rows[3])
    grad_visual = grad_visual + extra_vis
    grad_query = grad_query + extra_qry
    down_win, down_self = spread_grads(grad_visual, grad_query)
    mixed_grad_win, out_zero = output_back(mixed_win, down_win, weight_out[0])
    mixed_grad_self, out_one = output_back(mixed_self, down_self, weight_out[1])
    rows_win, in_zero = window_backward(
        full_win, weight_in[0], win_allowed, logit_scale, HD, offset, kept_win, mixed_grad_win
    )
    self_query, self_source, in_one = cross_backward(
        full_self,
        full_self,
        weight_in[1],
        self_allowed,
        logit_scale,
        HD,
        kept_self,
        mixed_grad_self,
    )
    settle_win, settle_self = settle_grads(rows_win, self_query + self_source)
    extra_vis, gain_zero = normalize_back(settle_win, unit_win, inv_win, gain_rows[0])
    extra_qry, gain_one = normalize_back(settle_self, unit_self, inv_self, gain_rows[1])
    grad_visual = grad_visual + extra_vis
    grad_query = grad_query + extra_qry
    grad_in = jnp.stack([in_zero, in_one, in_two, in_three])
    grad_out = jnp.stack([out_zero, out_one, out_two, out_three])
    grad_gain = jnp.stack([gain_zero, gain_one, gain_two, gain_three, gain_four, gain_five])
    sum_in, sum_out, sum_gain = (
        lax.psum_scatter(grad_in, "dp", scatter_dimension=1, tiled=True),
        lax.psum_scatter(grad_out, "dp", scatter_dimension=2, tiled=True),
        lax.psum_scatter(grad_gain, "dp", scatter_dimension=1, tiled=True),
    )
    sum_up, sum_down = (
        lax.psum_scatter(grad_up, "dp", scatter_dimension=1, tiled=True),
        lax.psum_scatter(grad_down, "dp", scatter_dimension=2, tiled=True),
    )
    total_gain = lax.psum(sum_gain, "tensor")
    return (
        visual_out.astype(jnp.bfloat16),
        query_out.astype(jnp.bfloat16),
        grad_visual.astype(jnp.bfloat16),
        grad_query.astype(jnp.bfloat16),
        sum_in,
        sum_out,
        sum_up,
        sum_down,
        total_gain,
    )


def solution(mesh):
    in_specs = (
        P(("dp", "tensor"), None),
        P(("dp", "tensor"), None),
        P("dp", None),
        P("dp", None),
        P("dp"),
        P(None, "dp", None, "tensor"),
        P(None, "tensor", "dp"),
        P(None, "dp", "tensor"),
        P(None, "tensor", "dp"),
        P(None, "dp"),
        P(("dp", "tensor"), None),
        P(("dp", "tensor"), None),
    )
    out_specs = (
        P(("dp", "tensor"), None),
        P(("dp", "tensor"), None),
        P(("dp", "tensor"), None),
        P(("dp", "tensor"), None),
        P(None, "dp", None, "tensor"),
        P(None, "tensor", "dp"),
        P(None, "dp", "tensor"),
        P(None, "tensor", "dp"),
        P(None, "dp"),
    )
    return jax.shard_map(
        on_device, mesh=mesh, in_specs=in_specs, out_specs=out_specs, check_vma=False
    )
```

profile of v0, /device:TPU:0, one launch (start us, length us, event | category | flops | bytes accessed | tf_op | source)
XLA Modules:
  0.0 1360.2 jit_solution(12029085750000062576)
XLA Ops:
  17.4 23.3 %all-gather = bf16[16,48,6]{1,2,0:T(8,128)(2,1)S(1)} all-gather(bf16[1,48,6]{1,2,0:T(8,128)(2,1)S(1)} %convert_bitcast_fusion), channel_id=1, replica_groups=mesh['dp'=16,'tensor'=2] {'dp'}, dimensions={0}, use_global_device_ids=true | all-gather | bytes 9792 | tf_op jit(solution)/shard_map/all_gather | solution.py:328
  41.7 10.7 all_gather.57
  54.8 11.6 all_gather.61
  66.4 13.9 %all-gather.6.cloned.1.call-done = bf16[4,768,3,384]{3,0,2,1:T(4,128)(2,1)} async-done(((bf16[4,48,3,384]{3,0,2,1:T(4,128)(2,1)}), bf16[4,768,3,384]{3,0,2,1:T(4,128)(2,1)}) %all-gather.6.cloned.1.call-update) | async-done | bytes 7077904 | tf_op jit(solution)/shard_map/all_gather | solution.py:324
  80.4 22.7 %fusion.339 = (bf16[1,768,3,384]{3,0,2,1:T(2,128)(2,1)}, bf16[1,768,3,384]{3,0,2,1:T(2,128)(2,1)}, bf16[1,768,3,384]{3,0,2,1:T(2,128)(2,1)}, bf16[1,768,3,384]{3,0,2,1:T(2,128)(2,1)}) fusion(bf16[4,768,3,384]{3,0,2,1:T(4,128)(2,1)} %all-gather.6.cloned.1.call-done), kind=kLoop, calls=%fused_computation.564 | loop fusion | bytes 14155776 | tf_op jit(solution)/shard_map/slice | solution.py:356
  130.4 12.6 while.112
  204.3 11.2 all_gather.62
  225.4 16.2 %while.110 = (s32[]{:T(128)}, bf16[6,1,432,64]{2,3,1,0:T(8,128)(2,1)}, f32[6,1,432,1]{2,3,1,0:T(1,128)S(1)}, bf16[6,1,432,64]{3,2,1,0:T(8,128)(2,1)S(1)}, bf16[6...) while((s32[]{:T(128)}, bf16[6,1,432,64]{2,3,1,0:T(8,128)(2,1)}, ...), condition=%wide.region_21.24_spmd, body=%wide.region_18.23_spmd.sunk | while | flops 58198608 | bytes 3112529 | solution.py:113
  248.5 17.1 %all_gather.67 = bf16[432,768]{1,0:T(8,128)(2,1)} all-gather(bf16[216,768]{1,0:T(8,128)(2,1)} %param.42), channel_id=1, replica_groups=mesh['dp'=16,'tensor'=2] {'tensor'}, dimensions={0}, use_global_device_ids=true | all-gather | bytes 995328 | tf_op jit(solution)/shard_map/all_gather | solution.py:284
  290.6 19.7 %while.114 = (s32[]{:T(128)}, bf16[6,1,512,64]{2,3,1,0:T(8,128)(2,1)S(1)}, f32[6,1,512,1]{2,3,1,0:T(1,128)S(1)}, bf16[6,1,512,64]{3,2,1,0:T(8,128)(2,1)S(1)}, bf...) while((s32[]{:T(128)}, ...), condition=%wide.region_29.32_spmd.clone, body=%wide.region_26.31_spmd.clone.sunk | while | flops 58428720 | bytes 3095565 | solution.py:113
  334.0 42.7 %all-gather.12.cloned.1.call-done = bf16[2,1536,768]{1,2,0:T(8,128)(2,1)} async-done(((bf16[2,1536,48]{1,2,0:T(8,128)(2,1)}), bf16[2,1536,768]{1,2,0:T(8,128)(2,1)}) %all-gather.12.cloned.1.call-update) | async-done | bytes 4718608 | tf_op jit(solution)/shard_map/all_gather | solution.py:327
  384.0 18.6 %all_gather.68 = bf16[512,768]{1,0:T(8,128)(2,1)} all-gather(bf16[256,768]{1,0:T(8,128)(2,1)S(1)} %copy-done.60), channel_id=1, replica_groups=mesh['dp'=16,'tensor'=2] {'tensor'}, dimensions={0}, use_global_device_ids=true | all-gather | bytes 1179648 | tf_op jit(solution)/shard_map/all_gather | solution.py:285
  408.6 19.0 %all_gather.66 = bf16[512,768]{1,0:T(8,128)(2,1)S(1)} all-gather(bf16[256,768]{1,0:T(8,128)(2,1)S(1)} %multiply_convert_fusion.4), channel_id=1, replica_groups=mesh['dp'=16,'tensor'=2] {'tensor'}, dimensions={0}, use_global_device_ids=true | all-gather | bytes 1179648 | tf_op jit(solution)/shard_map/all_gather | solution.py:267
  452.2 14.9 %all_gather.70 = bf16[432,768]{1,0:T(8,128)(2,1)S(1)} all-gather(bf16[216,768]{1,0:T(8,128)(2,1)S(1)} %get-tuple-element.858), channel_id=1, replica_groups=mesh['dp'=16,'tensor'=2] {'tensor'}, dimensions={0}, use_global_device_ids=true | all-gather | bytes 995328 | tf_op jit(solution)/shard_map/all_gather | solution.py:284
  471.3 39.3 %while.111 = (s32[]{:T(128)}, bf16[6,1,432,64]{2,3,1,0:T(8,128)(2,1)S(1)}, bf16[6,1,512,64]{2,3,1,0:T(8,128)(2,1)}, bf16[6,1,512,64]{2,3,1,0:T(8,128)(2,1)}, bf1...) while((s32[]{:T(128)}, ...), condition=%wide.region_45.48_spmd, body=%wide.region_43.47_spmd.sunk | while | flops 143480400 | bytes 7591465 | solution.py:157
  527.1 43.7 %while.115 = (s32[]{:T(128)}, bf16[6,1,512,64]{2,3,1,0:T(8,128)(2,1)S(1)}, bf16[6,1,432,64]{2,3,1,0:T(8,128)(2,1)}, bf16[6,1,432,64]{2,3,1,0:T(8,128)(2,1)}, bf1...) while((s32[]{:T(128)}, ...), condition=%wide.region_42.45_spmd.clone, body=%wide.region_40.44_spmd.clone.sunk | while | flops 143700272 | bytes 7704533 | solution.py:157
  597.2 15.6 %all_gather.71 = bf16[432,768]{1,0:T(8,128)(2,1)S(1)} all-gather(bf16[216,768]{1,0:T(8,128)(2,1)S(1)} %get-tuple-element.856), channel_id=1, replica_groups=mesh['dp'=16,'tensor'=2] {'tensor'}, dimensions={0}, use_global_device_ids=true | all-gather | bytes 995328 | tf_op jit(solution)/shard_map/all_gather | solution.py:284
  618.1 37.4 %while.116 = (s32[]{:T(128)}, bf16[6,3,144,64]{2,3,1,0:T(8,128)(2,1)S(1)}, bf16[6,3,144,64]{2,3,1,0:T(8,128)(2,1)S(1)}, bf16[6,3,144,64]{2,3,1,0:T(8,128)(2,1)},...) while((s32[]{:T(128)}, ...), condition=%wide.region_51.54_spmd.clone, body=%wide.region_49.53_spmd.clone.sunk | while | flops 40697424 | bytes 3492225 | solution.py:157
  676.8 15.7 %all_gather.72 = bf16[512,768]{1,0:T(8,128)(2,1)S(1)} all-gather(bf16[256,768]{1,0:T(8,128)(2,1)S(1)} %get-tuple-element.854), channel_id=1, replica_groups=mesh['dp'=16,'tensor'=2] {'tensor'}, dimensions={0}, use_global_device_ids=true | all-gather | bytes 1179648 | tf_op jit(solution)/shard_map/all_gather | solution.py:285
  694.9 37.2 %while.117 = (s32[]{:T(128)}, bf16[6,1,512,64]{2,3,1,0:T(8,128)(2,1)S(1)}, bf16[6,1,512,64]{2,3,1,0:T(8,128)(2,1)S(1)}, bf16[6,1,512,64]{2,3,1,0:T(8,128)(2,1)S(...) while((s32[]{:T(128)}, ...), condition=%wide.region_60.63_spmd.clone, body=%wide.region_58.62_spmd.clone.sunk | while | flops 170556928 | bytes 8998001 | solution.py:157
  744.2 15.0 %copy.135 = f32[2,1536,768]{1,0,2:T(2,128)} copy(f32[2,1536,768]{2,1,0:T(8,128)} %pad_maximum_fusion.2) | data formatting | bytes 18874368 | tf_op jit(solution)/shard_map/stack | solution.py:392
  832.1 254.4 %all-reduce.5.cloned.1.call-done = (f32[4,384,768]{1,0,2:T(4,128)}, f32[2,1536,768]{1,0,2:T(2,128)}) async-done(((f32[4,384,768]{1,0,2:T(4,128)}, f32[2,1536,768]{1,0,2:T(2,128)}), (f32[4,384,768]{1,0,2:T(4,128)}, f32[2,1536,768]{1,0,2:T(2,128)})) %all-reduce.5.cloned.1.call-update) | async-done | bytes 14155792
  1090.3 112.9 %reduce-scatter.44.cloned.1.call-done = f32[2,48,1536]{2,1,0:T(8,128)} async-done(((f32[2,768,1536]{2,1,0:T(8,128)}), f32[2,48,1536]{2,1,0:T(8,128)}) %reduce-scatter.44.cloned.1.call-update) | async-done | bytes 589840 | tf_op jit(solution)/shard_map/reduce_scatter | solution.py:444
  1203.2 150.0 %reduce-scatter.42.cloned.1.call-done = f32[4,48,3,384]{3,1,2,0:T(8,128)} async-done(((f32[4,768,3,384]{3,1,2,0:T(8,128)}), f32[4,48,3,384]{3,1,2,0:T(8,128)}) %reduce-scatter.42.cloned.1.call-update) | async-done | bytes 884752 | tf_op jit(solution)/shard_map/reduce_scatter | solution.py:439
  (780 shorter events, 574.7 us)
Async XLA Ops:
  7.2 73.2 %all-gather.6.cloned.1.call-start = ((), (), s32[]{:S(2)}) async-start(), calls=%async_computation.15 | async-start | bytes 7520256 | tf_op jit(solution)/shard_map/all_gather | solution.py:324
  9.6 135.3 %all-gather.8.cloned.1.call-start = ((), (), s32[]{:S(2)}) async-start(), calls=%async_computation.16 | async-start | bytes 2506752 | tf_op jit(solution)/shard_map/all_gather | solution.py:325
  11.3 173.2 %reduce-scatter.18.cloned.1.call-start = ((), (), s32[]{:S(2)}) async-start(), calls=%async_computation.17 | async-start | bytes 995328 | tf_op jit(solution)/shard_map/reduce_scatter | solution.py:273
  40.9 62.2 %copy-start.74 = (f32[768]{0:T(1024)}, f32[768]{0:T(1024)S(1)}, u32[]{:S(2)}) copy-start(f32[768]{0:T(1024)S(1)} %get-tuple-element.709) | copy-start | bytes 9220
  41.0 62.1 %copy-start.81 = (f32[216]{0:T(256)}, f32[216]{0:T(256)S(1)}, u32[]{:S(2)}) copy-start(f32[216]{0:T(256)S(1)} %broadcast_multiply_fusion.17) | copy-start | bytes 2596
  147.5 53.1 %reduce-scatter.20.cloned.1.call-start = ((), (), s32[]{:S(2)}) async-start(), calls=%async_computation.18 | async-start | bytes 1179648 | tf_op jit(solution)/shard_map/reduce_scatter | solution.py:276
  173.3 140.1 %reduce-scatter.22.cloned.1.call-start = ((), (), s32[]{:S(2)}) async-start(), calls=%async_computation.19 | async-start | bytes 995328 | tf_op jit(solution)/shard_map/reduce_scatter | solution.py:273
  215.5 72.4 %copy-start.13 = (bf16[512,768]{1,0:T(8,128)(2,1)}, bf16[512,768]{1,0:T(8,128)(2,1)S(1)}, u32[]{:S(2)}) copy-start(bf16[512,768]{1,0:T(8,128)(2,1)S(1)} %all_gather.62) | copy-start | bytes 2359300
  244.7 80.1 %all-gather.10.cloned.1.call-start = ((), (), s32[]{:S(2)}) async-start(), calls=%async_computation.20 | async-start | bytes 5013504 | tf_op jit(solution)/shard_map/all_gather | solution.py:326
  246.6 130.2 %all-gather.12.cloned.1.call-start = ((), (), s32[]{:S(2)}) async-start(), calls=%async_computation.21 | async-start | bytes 5013504 | tf_op jit(solution)/shard_map/all_gather | solution.py:327
  248.5 158.4 %reduce-scatter.26.cloned.1.call-start = ((), (), s32[]{:S(2)}) async-start(), calls=%async_computation.23 | async-start | bytes 1179648 | tf_op jit(solution)/shard_map/reduce_scatter | solution.py:276
  313.3 135.2 %reduce-scatter.30.cloned.1.call-start = ((), (), s32[]{:S(2)}) async-start(), calls=%async_computation.25 | async-start | bytes 995328 | tf_op jit(solution)/shard_map/reduce_scatter | solution.py:291
  383.9 66.0 %reduce-scatter.24.cloned.1.call-start = ((), (), s32[]{:S(2)}) async-start(), calls=%async_computation.22 | async-start | bytes 995328 | tf_op jit(solution)/shard_map/reduce_scatter | solution.py:273
  406.8 103.8 %reduce-scatter.32.cloned.1.call-start = ((), (), s32[]{:S(2)}) async-start(), calls=%async_computation.26 | async-start | bytes 1179648 | tf_op jit(solution)/shard_map/reduce_scatter | solution.py:294
  443.8 68.4 %reduce-scatter.28.cloned.1.call-start = ((), (), s32[]{:S(2)}) async-start(), calls=%async_computation.24 | async-start | bytes 1179648 | tf_op jit(solution)/shard_map/reduce_scatter | solution.py:276
  448.4 145.3 %reduce-scatter.34.cloned.1.call-start = ((), (), s32[]{:S(2)}) async-start(), calls=%async_computation.27 | async-start | bytes 995328 | tf_op jit(solution)/shard_map/reduce_scatter | solution.py:291
  510.6 63.9 %copy-start.26 = (bf16[6,1,432,64]{2,3,1,0:T(8,128)(2,1)}, bf16[6,1,432,64]{2,3,1,0:T(8,128)(2,1)S(1)}, u32[]{:S(2)}) copy-start(bf16[6,1,432,64]{2,3,1,0:T(8,128)(2,1)S(1)} %get-tuple-element.377) | copy-start | bytes 995332
  577.0 96.0 %reduce-scatter.38.cloned.1.call-start = ((), (), s32[]{:S(2)}) async-start(), calls=%async_computation.29 | async-start | bytes 1179648 | tf_op jit(solution)/shard_map/reduce_scatter | solution.py:294
  587.0 178.0 %reduce-scatter.36.cloned.1.call-start = ((), (), s32[]{:S(2)}) async-start(), calls=%async_computation.28 | async-start | bytes 995328 | tf_op jit(solution)/shard_map/reduce_scatter | solution.py:291
  673.0 94.0 %reduce-scatter.40.cloned.1.call-start = ((), (), s32[]{:S(2)}) async-start(), calls=%async_computation.30 | async-start | bytes 1179648 | tf_op jit(solution)/shard_map/reduce_scatter | solution.py:294
  736.0 89.8 %reduce-scatter.46.cloned.1.call-start = ((), (), s32[]{:S(2)}) async-start(), calls=%async_computation.33 | async-start | bytes 417792
  770.0 316.5 %all-reduce.5.cloned.1.call-start = ((), (), s32[]{:S(2)}) async-start(), calls=%async_computation.34 | async-start | bytes 28311552
  781.0 422.2 %reduce-scatter.44.cloned.1.call-start = ((), (), s32[]{:S(2)}) async-start(), calls=%async_computation.32 | async-start | bytes 10027008 | tf_op jit(solution)/shard_map/reduce_scatter | solution.py:444
  790.8 562.4 %reduce-scatter.42.cloned.1.call-start = ((), (), s32[]{:S(2)}) async-start(), calls=%async_computation.31 | async-start | bytes 15040512 | tf_op jit(solution)/shard_map/reduce_scatter | solution.py:439
  (101 other events, 839.0 us)
Sparse Core Ops, SparseCore 0:
  10.9 69.4 all-gather.5
  83.1 40.8 all-gather.7
  147.6 14.6 reduce-scatter.17
  173.4 16.0 reduce-scatter.19
  244.8 20.3 reduce-scatter.21
  268.2 53.3 all-gather.9
  324.7 52.0 all-gather.11
  379.1 22.5 reduce-scatter.25
  403.9 24.1 reduce-scatter.29
  430.3 16.1 reduce-scatter.23
  448.8 20.9 reduce-scatter.31
  471.9 17.7 reduce-scatter.27
  577.2 16.4 reduce-scatter.33
  595.8 21.3 reduce-scatter.37
  673.1 19.7 reduce-scatter.35
  736.1 17.4 reduce-scatter.39
  770.2 55.5 reduce-scatter.45
  830.3 256.1 all-reduce.4
  1091.7 111.3 reduce-scatter.43
  1207.8 145.3 reduce-scatter.41
where the time goes:
time: 1370 us; the launch traced here: 1360 us
  waiting for transfers between devices  587 us (43%)
  matrix products  290 us (21%)
  blocking collectives  192 us (14%)
  local copies, waits for them, and re-layouts  170 us (12%)
  other arithmetic  97.8 us (7%)
  between operations  20.4 us (1%)
    unnamed x22, waiting for transfers between devices  261 us
    reduce_scatter x1, waiting for transfers between devices, on_device(): lax.psum_scatter(grad_in, 'dp', scatter_dimension=1, tiled=True)  150 us
    reduce_scatter x1, waiting for transfers between devices, on_device(): lax.psum_scatter(grad_up, 'dp', scatter_dimension=1, tiled=True)  113 us
    unnamed x231, local copies, waits for them, and re-layouts  73.1 us
    dot_general x48, matrix products, one_head(): jnp.einsum('jty,joy->jto', per_head_queries, per_head_keys, preferred_ele...  49.5 us
    all_gather x3, blocking collectives, spread_grads(): lax.all_gather(first_grad.astype(jnp.bfloat16), 'tensor', axis=0, tiled=T...  47.6 us
    all_gather x1, waiting for transfers between devices, on_device(): lax.all_gather(master_down, 'dp', axis=2, tiled=True)  42.7 us
    all_gather x3, blocking collectives, spread_grads(): lax.all_gather(second_grad.astype(jnp.bfloat16), 'tensor', axis=0, tiled=...  42.7 us
  transfers between devices with their start and end apart: 20, of which 7 were waited for; matrix products, arithmetic and copies ran while one was open for 33% of the time, Pallas kernels for 0%

commit v1 on v0

v1 whole, which is shorter than its diff:
```python
import jax
import jax.numpy as jnp
from jax import lax
from jax.experimental import pallas as pl
from jax.experimental.pallas import tpu as pltpu
from jax.sharding import PartitionSpec as P

PH = 36
PW = 12
SCALE = 0.125
EPSILON = 1e-05
MASKED = -1e30
ROOT_HALF = 0.7071067811865476
INV_ROOT_TAU = 0.3989422804014327
F32 = jnp.float32
BF16 = jnp.bfloat16
WIDE = 1152
HALF = 384


def nn(a, b):
    return lax.dot_general(a, b, (((1,), (0,)), ((), ())), preferred_element_type=F32)


def nt(a, b):
    return lax.dot_general(a, b, (((1,), (1,)), ((), ())), preferred_element_type=F32)


def tn(a, b):
    return lax.dot_general(a, b, (((0,), (0,)), ((), ())), preferred_element_type=F32)


def unit_of(s):
    centred = s - jnp.mean(s, axis=-1, keepdims=True)
    inverse = lax.rsqrt(jnp.mean(centred * centred, axis=-1, keepdims=True) + EPSILON)
    return centred * inverse, inverse


def norm_back(dn, u, inverse, gain):
    scaled = dn * gain
    centre = jnp.mean(scaled, axis=-1, keepdims=True)
    slope = jnp.mean(scaled * u, axis=-1, keepdims=True)
    return inverse * (scaled - centre - u * slope)


def assemble(dst, own, other, t):
    half = own.shape[0]
    dst[pl.ds(pl.multiple_of(t * half, 8), half), :] = own[...].astype(F32)
    dst[pl.ds(pl.multiple_of((1 - t) * half, 8), half), :] = other[...].astype(F32)


def own_rows(ref, which, half):
    return ref[pl.ds(pl.multiple_of(which * half, 8), half), :]


def head_mask(h, value):
    lane = lax.broadcasted_iota(jnp.int32, (1, 128), 1)
    return jnp.where((lane >= 64) == (h == 1), value, 0.0).astype(BF16)


def twelfth(v):
    return lax.shift_right_logical(v * 43691, 19)


def places(shape, axis, scal):
    a, b = scal[1], scal[2]
    i = lax.broadcasted_iota(jnp.int32, shape, axis)
    r = twelfth(i)
    c = i - 12 * r
    rolled = jnp.where(r < a, r - a + PH, r - a)
    region = jnp.where(r < a, 2, 0) + jnp.where(c < b, 1, 0)
    return i, r, twelfth(rolled) * 4 + region


def window_bias(n, scal, key_axis):
    shape_k = (1, n) if key_axis == 1 else (n, 1)
    shape_q = (n, 1) if key_axis == 1 else (1, n)
    ik, rk, pk = places(shape_k, key_axis, scal)
    iq, _, pq = places(shape_q, 1 - key_axis, scal)
    usable = jnp.where(rk < scal[3], pk, -1)
    allowed = (usable == pq) | (ik == iq)
    return jnp.where(allowed, 0.0, MASKED).astype(F32)


def read_bias(n, scal, key_axis):
    shape = (1, n) if key_axis == 1 else (n, 1)
    i = lax.broadcasted_iota(jnp.int32, shape, key_axis)
    return jnp.where(twelfth(i) < scal[3], 0.0, MASKED).astype(F32)


def attend(q_ref, q_at, kv_ref, k_at, v_at, bias, o_ref):
    lane = lax.broadcasted_iota(jnp.int32, (1, 128), 1)
    for pair in range(3):
        at = pair * 128
        q = q_ref[:, q_at + at : q_at + at + 128]
        k = kv_ref[:, k_at + at : k_at + at + 128]
        v = kv_ref[:, v_at + at : v_at + at + 128]
        outs = []
        for h in range(2):
            s = nt(q * head_mask(h, SCALE), k)
            if bias is not None:
                s = s + bias
            e = jnp.exp(s - jnp.max(s, axis=1, keepdims=True))
            total = jnp.sum(e, axis=1, keepdims=True)
            outs.append(nn(e.astype(BF16), v) * (1.0 / total))
        o_ref[:, at : at + 128] = jnp.where(lane < 64, outs[0], outs[1]).astype(BF16)


def attend_back(q_ref, q_at, kv_ref, k_at, v_at, bias, do, dq_ref, dq_at, dk_ref, dk_at, dv_at):
    for pair in range(3):
        at = pair * 128
        q = q_ref[:, q_at + at : q_at + at + 128]
        k = kv_ref[:, k_at + at : k_at + at + 128]
        v = kv_ref[:, v_at + at : v_at + at + 128]
        dop = do[:, at : at + 128]
        dq, dk, dv = 0.0, 0.0, 0.0
        for h in range(2):
            keep = head_mask(h, 1.0)
            qm = q * head_mask(h, SCALE)
            dom = dop * keep
            s = nt(k, qm)
            if bias is not None:
                s = s + bias
            e = jnp.exp(s - jnp.max(s, axis=0, keepdims=True))
            p = e * (1.0 / jnp.sum(e, axis=0, keepdims=True))
            dp = nt(v, dom)
            delta = jnp.sum(p * dp, axis=0, keepdims=True)
            ds = (p * (dp - delta)).astype(BF16)
            dv = dv + nn(p.astype(BF16), dom)
            dk = dk + nn(ds, qm)
            dq = dq + tn(ds, k * keep)
        dq_ref[:, dq_at + at : dq_at + at + 128] = (dq * SCALE).astype(BF16)
        dk_ref[:, dk_at + at : dk_at + at + 128] = dk.astype(BF16)
        dk_ref[:, dv_at + at : dv_at + at + 128] = dv.astype(BF16)


def first_kernel(windowed, index, *refs):
    if windowed:
        scal, own, other, gains, w, s_ref, n_ref, qkv, o_ref, gr_ref = refs
    else:
        scal, own, other, gains, w, seg_c, seg_r, s_ref, n_ref, qkv, o_ref = refs
    assemble(s_ref, own, other, scal[0])
    gr = gains[...].astype(F32).T[0:8, :]
    if windowed:
        gr_ref[...] = gr
    u, _ = unit_of(s_ref[...])
    n = (u * gr[index : index + 1, :]).astype(BF16)
    n_ref[...] = n
    qkv[...] = nn(n, w[...]).astype(BF16)
    if windowed:
        bias = window_bias(qkv.shape[0], scal, 1)
    else:
        bias = jnp.where(seg_c[...] == seg_r[...], 0.0, MASKED).astype(F32)
    attend(qkv, 0, qkv, HALF, 2 * HALF, bias, o_ref)


def middle_kernel(index, s, o_own, o_oth, ao_own, ao_oth, gr, w, s1, n_ref, proj):
    branch = nt(o_own[...], ao_own[...]) + nt(o_oth[...], ao_oth[...])
    stream = s[...] + branch
    s1[...] = stream
    u, _ = unit_of(stream)
    n = (u * gr[index : index + 1, :]).astype(BF16)
    n_ref[...] = n
    proj[...] = nn(n, w[...]).astype(BF16)


def cross_kernel(masked, scal, q_ref, kv_ref, o_ref):
    bias = read_bias(kv_ref.shape[0], scal, 1) if masked else None
    attend(q_ref, 0, kv_ref, HALF, 2 * HALF, bias, o_ref)


def mlp_kernel(index, steps, scal, s1, o_own, o_oth, ao_own, ao_oth, gr, cot_own, cot_oth, w_in, w_out,
               s2, send, keep, dn_ref, dg_ref, dm_ref, n_s, dy_s, nt_s, dyt_s, part_s, dn_s, cot_s):
    step = pl.program_id(0)
    half = cot_own.shape[0]
    t = scal[0]

    @pl.when(step == 0)
    def _():
        branch = nt(o_own[...], ao_own[...]) + nt(o_oth[...], ao_oth[...])
        stream = s1[...] + branch
        s2[...] = stream
        u, _ = unit_of(stream)
        n = (u * gr[index : index + 1, :]).astype(BF16)
        n_s[...] = n
        nt_s[...] = n.T
        assemble(cot_s, cot_own, cot_oth, t)
        dy = cot_s[...].astype(BF16)
        dy_s[...] = dy
        dyt_s[...] = dy.T

    hidden = nn(n_s[...], w_in[...])
    phi = 0.5 * (1.0 + lax.erf(hidden * ROOT_HALF))
    act = (hidden * phi).astype(BF16)
    slope = phi + hidden * jnp.exp(-0.5 * hidden * hidden) * INV_ROOT_TAU
    dh = (nn(dy_s[...], w_out[...]) * slope).astype(BF16)
    part = nt(act, w_out[...])
    dn = nt(dh, w_in[...])

    @pl.when(step == 0)
    def _():
        part_s[...] = part
        dn_s[...] = dn

    @pl.when(step > 0)
    def _():
        part_s[...] += part
        dn_s[...] += dn

    fb = w_in.shape[1]
    dm_ref[:, 0:fb] = nn(nt_s[...], dh).astype(BF16)
    dm_ref[:, fb : 2 * fb] = nn(dyt_s[...], act).astype(BF16)

    @pl.when(step == steps - 1)
    def _():
        send[...] = own_rows(part_s, 1 - t, half).astype(BF16)
        keep[...] = own_rows(part_s, t, half) + own_rows(s2, t, half)
        dn_all = dn_s[...]
        dn_ref[...] = dn_all.astype(BF16)
        u, _ = unit_of(s2[...])
        dg_ref[...] = jnp.sum(dn_all * u, axis=0, keepdims=True)


def cross_back_kernel(masked, index, scal, cot_own, cot_oth, dn_own, dn_oth, s2, gr, ao_own, q_ref, kv_ref,
                      g_ref, dy_ref, dq_ref, dkv_ref):
    assemble(g_ref, cot_own, cot_oth, scal[0])
    u, inverse = unit_of(s2[...])
    dn = dn_own[...].astype(F32) + dn_oth[...].astype(F32)
    grad = g_ref[...] + norm_back(dn, u, inverse, gr[index : index + 1, :])
    g_ref[...] = grad
    dy = grad.astype(BF16)
    dy_ref[...] = dy
    do = nn(dy, ao_own[...]).astype(BF16)
    bias = read_bias(kv_ref.shape[0], scal, 0) if masked else None
    attend_back(q_ref, 0, kv_ref, HALF, 2 * HALF, bias, do, dq_ref, 0, dkv_ref, 0, HALF)


def dn_kernel(dq, dkv, w, s1, dn_ref, dg_ref):
    dn = nt(dq[...], w[:, 0:HALF]) + nt(dkv[...], w[:, HALF:WIDE])
    dn_ref[...] = dn.astype(BF16)
    u, _ = unit_of(s1[...])
    dg_ref[...] = jnp.sum(dn * u, axis=0, keepdims=True)


def middle_weights_kernel(nv, nq, dq3, dkv2, dq2, dkv3, dyv, o_look, dyq, o_read, out):
    out[:, 0:HALF] = tn(nv[...], dq3[...]).astype(BF16)
    out[:, HALF:WIDE] = tn(nv[...], dkv2[...]).astype(BF16)
    out[:, WIDE : WIDE + HALF] = tn(nq[...], dq2[...]).astype(BF16)
    out[:, WIDE + HALF : 2 * WIDE] = tn(nq[...], dkv3[...]).astype(BF16)
    out[:, 2 * WIDE : 2 * WIDE + HALF] = tn(dyq[...], o_read[...]).astype(BF16)
    out[:, 2 * WIDE + HALF : 2 * WIDE + 2 * HALF] = tn(dyv[...], o_look[...]).astype(BF16)


def first_back_kernel(windowed, index, later, scal, *refs):
    if windowed:
        grad, dn_own, dn_oth, s1, s0, gr, ao_own, w, qkv, g_ref, dy_ref, dqkv, send, keep, dg_ref, g_s = refs
    else:
        (grad, dn_own, dn_oth, s1, s0, gr, ao_own, w, qkv, seg_c, seg_r,
         g_ref, dy_ref, dqkv, send, keep, dg_ref, g_s) = refs
    t = scal[0]
    half = g_ref.shape[0]
    u, inverse = unit_of(s1[...])
    dn = dn_own[...].astype(F32) + dn_oth[...].astype(F32)
    g = grad[...] + norm_back(dn, u, inverse, gr[later : later + 1, :])
    g_s[...] = g
    g_ref[...] = own_rows(g_s, t, half)
    dy = g.astype(BF16)
    dy_ref[...] = dy
    do = nn(dy, ao_own[...]).astype(BF16)
    if windowed:
        bias = window_bias(qkv.shape[0], scal, 0)
    else:
        bias = jnp.where(seg_c[...] == seg_r[...], 0.0, MASKED).astype(F32)
    attend_back(qkv, 0, qkv, HALF, 2 * HALF, bias, do, dqkv, 0, dqkv, HALF, 2 * HALF)
    dn0 = nt(dqkv[...], w[...])
    g_s[...] = dn0
    send[...] = own_rows(g_s, 1 - t, half).astype(BF16)
    keep[...] = own_rows(g_s, t, half)
    u, _ = unit_of(s0[...])
    dg_ref[...] = jnp.sum(dn0 * u, axis=0, keepdims=True)


def first_weights_kernel(n0, n1, d0, d1, dy0, o0, dy1, o1, g0, g1, g2, g3, g4, g5, out, rows):
    out[:, 0:WIDE] = tn(n0[...], d0[...]).astype(BF16)
    out[:, WIDE : 2 * WIDE] = tn(n1[...], d1[...]).astype(BF16)
    out[:, 2 * WIDE : 2 * WIDE + HALF] = tn(dy0[...], o0[...]).astype(BF16)
    out[:, 2 * WIDE + HALF : 2 * WIDE + 2 * HALF] = tn(dy1[...], o1[...]).astype(BF16)
    rows[...] = jnp.zeros_like(rows)
    for i, g in enumerate((g0, g1, g2, g3, g4, g5)):
        rows[i : i + 1, :] = g[...]
    out[:, 2 * WIDE + 2 * HALF :] = rows[...].T.astype(BF16)


def last_kernel(index, grad, keep, got, own, gr, out):
    u, inverse = unit_of(own[...].astype(F32))
    dn = keep[...] + got[...].astype(F32)
    out[...] = (grad[...] + norm_back(dn, u, inverse, gr[index : index + 1, :])).astype(BF16)


SMEM = pl.BlockSpec(memory_space=pltpu.SMEM)
FULL = None


def call(body, args, specs, outs, name, flops, scratch=(), grid=(1,), out_specs=None):
    def whole(shape):
        return pl.BlockSpec(shape, lambda *_: (0,) * len(shape))

    in_specs = [whole(a.shape) if s is FULL else s for a, s in zip(args, specs)]
    out_specs = [whole(o.shape) if s is FULL else s for o, s in zip(outs, out_specs or [FULL] * len(outs))]
    moved = sum(a.size * a.dtype.itemsize for a in outs)
    for a, s in zip(args, in_specs):
        size = a.size if s.block_shape is None else min(a.size, s.block_shape[0] * s.block_shape[1] * grid[0])
        moved += size * a.dtype.itemsize
    return pl.pallas_call(
        body,
        out_shape=outs,
        grid=grid,
        in_specs=in_specs,
        out_specs=out_specs,
        scratch_shapes=list(scratch),
        name=name,
        compiler_params=pltpu.CompilerParams(vmem_limit_bytes=56 * 2**20),
        cost_estimate=pl.CostEstimate(flops=int(flops), bytes_accessed=int(moved), transcendentals=0),
    )(*args)


def cols(width, at):
    return pl.BlockSpec((768, width), lambda *_: (0, at))


def part(body, *fixed):
    return lambda *refs: body(*fixed, *refs)


def sds(shape, dtype):
    return jax.ShapeDtypeStruct(shape, dtype)


def on_device(visual, query, seg_ids, shifts, valid_rows, attn_in, attn_out, mlp_in, mlp_out, gains, cot_visual, cot_query):
    def swap(a):
        return lax.ppermute(a, "tensor", [(0, 1), (1, 0)])

    def gather(a):
        return lax.all_gather(a, "dp", axis=0, tiled=True)

    def scatter(a):
        return lax.psum_scatter(a, "dp", scatter_dimension=0, tiled=True)

    depth = gains.shape[1]
    rv, rq = 2 * visual.shape[0], 2 * query.shape[0]
    t = lax.axis_index("tensor").astype(jnp.int32)
    scal = jnp.concatenate([t[None], shifts[0], valid_rows])
    seg_r = seg_ids
    seg_c = seg_ids.reshape(-1, 1)

    x_oth, q_oth = swap(visual), swap(query)
    a_in = attn_in.astype(BF16)
    gain_cols = jnp.pad(gains.T.astype(BF16), ((0, 0), (0, 122)))
    g1 = gather(jnp.concatenate([a_in[0].reshape(depth, WIDE), a_in[1].reshape(depth, WIDE), gain_cols], axis=1))
    aot = attn_out.astype(BF16).transpose(2, 0, 1).reshape(depth, 4 * HALF)
    aot = gather(jnp.concatenate([aot, swap(aot)], axis=1))
    g2 = gather(jnp.concatenate([a_in[3][:, 0], a_in[2][:, 1], a_in[2][:, 2], a_in[2][:, 0], a_in[3][:, 1], a_in[3][:, 2]], axis=1))
    m_in = mlp_in.astype(BF16)
    m_out = mlp_out.astype(BF16).transpose(0, 2, 1)
    g3 = gather(jnp.concatenate([m_in[0], m_out[0], m_in[1], m_out[1]], axis=1))
    cv_oth, cq_oth = swap(cot_visual), swap(cot_query)

    def first(windowed, own, other, at, rows):
        args = [scal, own, other, g1, g1]
        specs = [SMEM, FULL, FULL, cols(128, 18), cols(WIDE, at)]
        outs = [sds((rows, 768), F32), sds((rows, 768), BF16), sds((rows, WIDE), BF16), sds((rows, HALF), BF16)]
        if windowed:
            outs.append(sds((8, 768), F32))
        else:
            args += [seg_c, seg_r]
            specs += [FULL, FULL]
        return call(part(first_kernel, windowed, at), args, specs, outs, "first_%d" % at, 4e9)

    sv0, nv0, qkv0, o0, gr = first(True, visual, x_oth, 0, rv)
    o0_oth = swap(o0)
    sq0, nq0, qkv1, o1 = first(False, query, q_oth, 1, rq)
    o1_oth = swap(o1)

    def middle(index, s, o, o_oth, a, at, rows):
        return call(
            part(middle_kernel, index), [s, o, o_oth, aot, aot, gr, g2],
            [FULL, FULL, FULL, cols(HALF, a), cols(HALF, 4 + a), FULL, cols(WIDE, at)],
            [sds((rows, 768), F32), sds((rows, 768), BF16), sds((rows, WIDE), BF16)], "middle_%d" % at, 2e9)

    sv1, nv, pv = middle(2, sv0, o0, o0_oth, 0, 0, rv)
    sq1, nq, pq = middle(3, sq0, o1, o1_oth, 1, 1, rq)

    def cross(masked, q, kv, name):
        return call(part(cross_kernel, masked), [scal, q, kv], [SMEM, FULL, FULL], [sds((q.shape[0], HALF), BF16)], name, 2e9)[0]

    o3 = cross(False, pv, pq, "look")
    o3_oth = swap(o3)
    o2 = cross(True, pq, pv, "read")
    o2_oth = swap(o2)

    fb = 512
    steps = 1536 // fb

    def mlp(index, s1, o, o_oth, a, cot, cot_oth, m, rows):
        half = rows // 2

        def block(at):
            return pl.BlockSpec((768, fb), lambda i: (0, at * steps + i))

        return call(
            part(mlp_kernel, index, steps), [scal, s1, o, o_oth, aot, aot, gr, cot, cot_oth, g3, g3],
            [SMEM, FULL, FULL, FULL, cols(HALF, a), cols(HALF, 4 + a), FULL, FULL, FULL, block(2 * m), block(2 * m + 1)],
            [sds((rows, 768), F32), sds((half, 768), BF16), sds((half, 768), F32), sds((rows, 768), BF16),
             sds((1, 768), F32), sds((768, 3072), BF16)], "mlp_%d" % m, 10 * rows * 768 * 1536,
            scratch=[pltpu.VMEM((rows, 768), BF16), pltpu.VMEM((rows, 768), BF16), pltpu.VMEM((768, rows), BF16),
                     pltpu.VMEM((768, rows), BF16), pltpu.VMEM((rows, 768), F32), pltpu.VMEM((rows, 768), F32),
                     pltpu.VMEM((rows, 768), F32)],
            grid=(steps,), out_specs=[FULL] * 5 + [pl.BlockSpec((768, 2 * fb), lambda i: (0, i))])

    sv2, part_v, keep_v, dnv4, dg4, dm0 = mlp(4, sv1, o3, o3_oth, 3, cot_visual, cv_oth, 0, rv)
    dnv4_oth = swap(dnv4)
    sq2, part_q, keep_q, dnq5, dg5, dm1 = mlp(5, sq1, o2, o2_oth, 2, cot_query, cq_oth, 1, rq)
    dnq5_oth = swap(dnq5)
    s3v, s3q = scatter(dm0), scatter(dm1)
    out_visual = (keep_v + swap(part_v).astype(F32)).astype(BF16)
    out_query = (keep_q + swap(part_q).astype(F32)).astype(BF16)

    def cross_back(masked, index, cot, cot_oth, dn, dn_oth, s2, a, q, kv, name):
        return call(
            part(cross_back_kernel, masked, index), [scal, cot, cot_oth, dn, dn_oth, s2, gr, aot, q, kv],
            [SMEM, FULL, FULL, FULL, FULL, FULL, FULL, cols(HALF, a), FULL, FULL],
            [sds((q.shape[0], 768), F32), sds((q.shape[0], 768), BF16), sds((q.shape[0], HALF), BF16), sds((kv.shape[0], 768), BF16)],
            name, 6e9)

    gv2, dyv, dq3, dkv3 = cross_back(False, 4, cot_visual, cv_oth, dnv4, dnv4_oth, sv2, 3, pv, pq, "look_back")
    gq2, dyq, dq2, dkv2 = cross_back(True, 5, cot_query, cq_oth, dnq5, dnq5_oth, sq2, 2, pq, pv, "read_back")

    def dn_of(dq, dkv, at, s1, rows):
        return call(dn_kernel, [dq, dkv, g2, s1], [FULL, FULL, cols(WIDE, at), FULL],
                    [sds((rows, 768), BF16), sds((1, 768), F32)], "dn_%d" % at, 1e9)

    dnv2, dg2 = dn_of(dq3, dkv2, 0, sv1, rv)
    dnv2_oth = swap(dnv2)
    dnq3, dg3 = dn_of(dq2, dkv3, 1, sq1, rq)
    dnq3_oth = swap(dnq3)
    args = [nv, nq, dq3, dkv2, dq2, dkv3, dyv, o3, dyq, o2]
    (dw2,) = call(middle_weights_kernel, args, [FULL] * len(args), [sds((768, 2 * WIDE + 2 * HALF), BF16)], "middle_weights", 2.5e9)
    s2 = scatter(dw2)

    def first_back(windowed, index, later, grad, dn, dn_oth, s1, s0, a, qkv, rows):
        half = rows // 2
        args = [scal, grad, dn, dn_oth, s1, s0, gr, aot, g1, qkv]
        specs = [SMEM, FULL, FULL, FULL, FULL, FULL, FULL, cols(HALF, a), cols(WIDE, a), FULL]
        if not windowed:
            args += [seg_c, seg_r]
            specs += [FULL, FULL]
        outs = [sds((half, 768), F32), sds((rows, 768), BF16), sds((rows, WIDE), BF16), sds((half, 768), BF16),
                sds((half, 768), F32), sds((1, 768), F32)]
        return call(part(first_back_kernel, windowed, index, later), args, specs, outs, "first_back_%d" % a, 7e9,
                    scratch=[pltpu.VMEM((rows, 768), F32)])

    gv1, dy0, d0, send_v, hold_v, dg0 = first_back(True, 0, 2, gv2, dnv2, dnv2_oth, sv1, sv0, 0, qkv0, rv)
    got_v = swap(send_v)
    gq1, dy1, d1, send_q, hold_q, dg1 = first_back(False, 1, 3, gq2, dnq3, dnq3_oth, sq1, sq0, 1, qkv1, rq)
    got_q = swap(send_q)
    args = [nv0, nq0, d0, d1, dy0, o0, dy1, o1, dg0, dg1, dg2, dg3, dg4, dg5]
    (dw1,) = call(first_weights_kernel, args, [FULL] * len(args), [sds((768, 2 * WIDE + 2 * HALF + 128), BF16)],
                  "first_weights", 3e9, scratch=[pltpu.VMEM((128, 768), F32)])
    s1 = scatter(dw1)

    def last(index, grad, keep, got, own):
        return call(part(last_kernel, index), [grad, keep, got, own, gr], [FULL] * 5, [sds(own.shape, BF16)], "last_%d" % index, 1e7)[0]

    grad_visual = last(0, gv1, hold_v, got_v, visual)
    grad_query = last(1, gq1, hold_q, got_q, query)

    def slots(a):
        return a.reshape(depth, 3, HALF)

    v2, q2 = slots(s2[:, 0:WIDE]), slots(s2[:, WIDE : 2 * WIDE])
    in2 = jnp.stack([q2[:, 0], v2[:, 1], v2[:, 2]], axis=1)
    in3 = jnp.stack([v2[:, 0], q2[:, 1], q2[:, 2]], axis=1)
    grad_in = jnp.stack([slots(s1[:, 0:WIDE]), slots(s1[:, WIDE : 2 * WIDE]), in2, in3]).astype(F32)
    base = 2 * WIDE
    grad_out = jnp.stack([s1[:, base : base + HALF].T, s1[:, base + HALF : base + 2 * HALF].T,
                          s2[:, base : base + HALF].T, s2[:, base + HALF : base + 2 * HALF].T]).astype(F32)
    m3 = jnp.stack([s3v, s3q]).reshape(2, depth, steps, 2, fb)
    grad_up = m3[:, :, :, 0].reshape(2, depth, 1536).astype(F32)
    grad_down = m3[:, :, :, 1].reshape(2, depth, 1536).transpose(0, 2, 1).astype(F32)
    gsum = s1[:, base + 2 * HALF :].astype(F32)
    gsum = gsum + swap(gsum)
    grad_gain = gsum[:, 0:6].T
    return out_visual, out_query, grad_visual, grad_query, grad_in, grad_out, grad_up, grad_down, grad_gain


def solution(mesh):
    rows = P(("dp", "tensor"), None)
    weights = (P(None, "dp", None, "tensor"), P(None, "tensor", "dp"), P(None, "dp", "tensor"), P(None, "tensor", "dp"), P(None, "dp"))
    in_specs = (rows, rows, P("dp", None), P("dp", None), P("dp")) + weights + (rows, rows)
    out_specs = (rows, rows, rows, rows) + weights
    return jax.shard_map(on_device, mesh=mesh, in_specs=in_specs, out_specs=out_specs, check_vma=False)
```

time: 1370 us -> 600 us (0.44)
  matrix products: 290 us -> 0 us
  waiting for transfers between devices: 587 us -> 372 us
  blocking collectives: 192 us -> 0 us
  local copies, waits for them, and re-layouts: 170 us -> 22.8 us
  Pallas kernels: 0 us -> 145 us
  other arithmetic: 97.8 us -> 12.5 us
  starting transfers between devices: 1.43 us -> 22 us
    dot_general x213 -> x0, matrix products: 290 us -> none  [the longest x48 49.5 us: one_head(): jnp.einsum('jty,joy->jto', per_head_queries, per_head_keys, preferred_ele...]
    unnamed x22 -> x8, waiting for transfers between devices: 261 us -> 0.13 us
    all_gather x13 -> x0, blocking collectives: 187 us -> none  [the longest x3 47.6 us: spread_grads(): lax.all_gather(first_grad.astype(jnp.bfloat16), 'tensor', axis=0, tiled=T...]
    reduce_scatter x14 -> x4, waiting for transfers between devices: 270 us -> 112 us  [scatter(): return lax.psum_scatter(a, 'dp', scatter_dimension=0, tiled=True)]
    pallas_call x0 -> x18, Pallas kernels: none -> 145 us  [call(): pl.pallas_call(body, out_shape=outs, grid=grid, in_specs=in_specs, out_sp...]
    all_gather x4, waiting for transfers between devices: 56.7 us -> 173 us  [gather(): return lax.all_gather(a, 'dp', axis=0, tiled=True)]
    ppermute x0 -> x18, waiting for transfers between devices: none -> 86.8 us  [swap(): return lax.ppermute(a, 'tensor', [(0, 1), (1, 0)])]
    unnamed x231 -> x74, local copies, waits for them, and re-layouts: 73.1 us -> 12.5 us
  transfers between devices with their start and end apart: 20 -> 26, of which waited for: 7 -> 19; matrix products, arithmetic and copies ran while one was open for 33% -> 3% of each run, Pallas kernels for 0% -> 22%
where the time goes in v1:
time: 600 us; the launch traced here: 590 us
  waiting for transfers between devices  372 us (62%)
  Pallas kernels  145 us (24%)
  local copies, waits for them, and re-layouts  22.8 us (4%)
  starting transfers between devices  22 us (4%)
  between operations  15.5 us (3%)
  other arithmetic  12.5 us (2%)
    all_gather x4, waiting for transfers between devices, gather(): return lax.all_gather(a, 'dp', axis=0, tiled=True)  173 us
    pallas_call x18, Pallas kernels, call(): pl.pallas_call(body, out_shape=outs, grid=grid, in_specs=in_specs, out_sp...  145 us
    reduce_scatter x4, waiting for transfers between devices, scatter(): return lax.psum_scatter(a, 'dp', scatter_dimension=0, tiled=True)  112 us
    ppermute x18, waiting for transfers between devices, swap(): return lax.ppermute(a, 'tensor', [(0, 1), (1, 0)])  86.8 us
    ppermute x18, starting transfers between devices, swap(): return lax.ppermute(a, 'tensor', [(0, 1), (1, 0)])  21.5 us
    unnamed x74, local copies, waits for them, and re-layouts  12.5 us
  transfers between devices with their start and end apart: 26, of which 19 were waited for; matrix products, arithmetic and copies ran while one was open for 3% of the time, Pallas kernels for 22%

profile of v1, /device:TPU:0, one launch (start us, length us, event | category | flops | bytes accessed | tf_op | source)
XLA Modules:
  0.0 590.0 jit_solution(8362628701769861607)
XLA Ops:
  24.3 6.5 %collective-permute-done.refs_2_ = bf16[216,768]{1,0:T(8,128)(2,1)S(1)} collective-permute-done((bf16[216,768]{1,0:T(8,128)(2,1)S(1)}, bf16[216,768]{1,0:T(8,128)(2,1)S(1)}, u32[]{:S(2)}, u32[]{:S(2)}) %collective-permute-start) | collective-permute-done | bytes 331808 | tf_op jit(solution)/shard_map/ppermute | solution.py:341
  30.8 30.5 %all-gather.5.cloned.1.call-done.refs_3_.refs_4_.refs_8_ = bf16[768,2432]{1,0:T(8,128)(2,1)} async-done(((bf16[48,2432]{1,0:T(8,128)(2,1)}), bf16[768,2432]{1,0:T(8,128)(2,1)}) %all-gather.5.cloned.1.call-update) | async-done | bytes 3735568 | tf_op jit(solution)/shard_map/all_gather | solution.py:344
  69.4 6.5 %first_1.1 = (f32[512,768]{1,0:T(8,128)}, bf16[512,768]{1,0:T(8,128)(2,1)}, bf16[512,1152]{1,0:T(8,128)(2,1)}, bf16[512,384]{1,0:T(8,128)(2,1)}) custom-call(s32[4]{0:T(128)} %pad_add_fusion.refs_0_, bf16[256,768]{1,0:T(8,128)(2,1)} %refs_3_.3, bf16[256,768]{1,0:T(8,128)(2,1)} %copy-done.28, ...), custom_call_target="tpu_custom_call" | custom-call | flops 4000000000 | bytes 6688784 | tf_op jit(solution)/shard_map/first_1/pallas_call | solution.py:314
  77.9 32.6 %all-gather.9.cloned.1.call-done.refs_6_.w = bf16[768,2304]{1,0:T(8,128)(2,1)} async-done(((bf16[48,2304]{1,0:T(8,128)(2,1)}), bf16[768,2304]{1,0:T(8,128)(2,1)}) %all-gather.9.cloned.1.call-update) | async-done | bytes 3538960 | tf_op jit(solution)/shard_map/all_gather | solution.py:344
  110.4 55.3 %all-gather.7.cloned.1.call-done.refs_3_.refs_4_.refs_5_.refs_7_ = bf16[768,3072]{1,0:T(8,128)(2,1)} async-done(((bf16[48,3072]{1,0:T(8,128)(2,1)}), bf16[768,3072]{1,0:T(8,128)(2,1)}) %all-gather.7.cloned.1.call-update) | async-done | bytes 4718608 | tf_op jit(solution)/shard_map/all_gather | solution.py:344
  172.3 6.6 %middle_1.1 = (f32[512,768]{1,0:T(8,128)}, bf16[512,768]{1,0:T(8,128)(2,1)}, bf16[512,1152]{1,0:T(8,128)(2,1)}) custom-call(f32[512,768]{1,0:T(8,128)} %get-tuple-element.65.refs_0_.refs_5_, bf16[512,384]{1,0:T(8,128)(2,1)} %get-tuple-element.66.refs_1_.o1, bf16[512,384]{1,0:T(8,128)(2,1)} %copy-done.9, ...), custom_call_target="tpu_custom_call" | custom-call | flops 2000000000 | bytes 8871936 | tf_op jit(solution)/shard_map/middle_1/pallas_call | solution.py:314
  184.9 8.8 %collective-permute-done.5.refs_3_ = bf16[432,384]{1,0:T(8,128)(2,1)S(1)} collective-permute-done((bf16[432,384]{1,0:T(8,128)(2,1)}, bf16[432,384]{1,0:T(8,128)(2,1)S(1)}, u32[]{:S(2)}, u32[]{:S(2)}) %collective-permute-start.5) | collective-permute-done | bytes 331808 | tf_op jit(solution)/shard_map/ppermute | solution.py:341
  193.7 54.8 %all-gather.11.cloned.1.call-done.refs_9_.refs_10_ = bf16[768,6144]{1,0:T(8,128)(2,1)} async-done(((bf16[48,6144]{1,0:T(8,128)(2,1)}), bf16[768,6144]{1,0:T(8,128)(2,1)}) %all-gather.11.cloned.1.call-update) | async-done | bytes 9437200 | tf_op jit(solution)/shard_map/all_gather | solution.py:344
  248.5 15.4 %mlp_0.1 = (f32[432,768]{1,0:T(8,128)}, bf16[216,768]{1,0:T(8,128)(2,1)}, f32[216,768]{1,0:T(8,128)}, bf16[432,768]{1,0:T(8,128)(2,1)}, f32[1,768]{1,0:T(1,128)}, /*index=5*/bf16[768,3072]{1,0:T(8,128)(2,1)}) custom-call(s32[4]{0:T(128)} %pad_add_fusion.refs_0_, f32[432,768]{1,0:T(8,128)} %get-tuple-element.63.refs_1_.s1.refs_4_, ...), custom_call_target="tpu_custom_call" | custom-call | flops 5096079360 | bytes 18643984 | tf_op jit(solution)/shard_map/mlp_0/pallas_call | solution.py:314
  276.8 7.8 %collective-permute-done.8.refs_3_ = bf16[512,384]{1,0:T(8,128)(2,1)S(1)} collective-permute-done((bf16[512,384]{1,0:T(8,128)(2,1)}, bf16[512,384]{1,0:T(8,128)(2,1)S(1)}, u32[]{:S(2)}, u32[]{:S(2)}) %collective-permute-start.8) | collective-permute-done | bytes 393248 | tf_op jit(solution)/shard_map/ppermute | solution.py:341
  285.3 16.8 %mlp_1.1 = (f32[512,768]{1,0:T(8,128)}, bf16[256,768]{1,0:T(8,128)(2,1)}, f32[256,768]{1,0:T(8,128)}, bf16[512,768]{1,0:T(8,128)(2,1)}, f32[1,768]{1,0:T(1,128)}, /*index=5*/bf16[768,3072]{1,0:T(8,128)(2,1)}) custom-call(s32[4]{0:T(128)} %pad_add_fusion.refs_0_, f32[512,768]{1,0:T(8,128)} %get-tuple-element.70.refs_1_.s1.refs_4_, ...), custom_call_target="tpu_custom_call" | custom-call | flops 6039797760 | bytes 19688464 | tf_op jit(solution)/shard_map/mlp_1/pallas_call | solution.py:314
  305.2 15.8 %collective-permute-done.11.refs_4_ = bf16[432,768]{1,0:T(8,128)(2,1)S(1)} collective-permute-done((bf16[432,768]{1,0:T(8,128)(2,1)S(1)}, bf16[432,768]{1,0:T(8,128)(2,1)S(1)}, u32[]{:S(2)}, u32[]{:S(2)}) %collective-permute-start.11) | collective-permute-done | bytes 663584 | tf_op jit(solution)/shard_map/ppermute | solution.py:341
  321.9 10.8 %look_back.1 = (f32[432,768]{1,0:T(8,128)}, bf16[432,768]{1,0:T(8,128)(2,1)}, bf16[432,384]{1,0:T(8,128)(2,1)}, bf16[512,768]{1,0:T(8,128)(2,1)}) custom-call(s32[4]{0:T(128)} %pad_add_fusion.refs_0_, bf16[216,768]{1,0:T(8,128)(2,1)} %refs_1_.6, bf16[216,768]{1,0:T(8,128)(2,1)} %copy-done.11, bf16[432,768]{1,0:T(8,128)(2,1)} %get-tuple-element.73.refs_3_, ...), custom_call_target="tpu_custom_call" | custom-call | flops 6000000000 | bytes 9216016 | tf_op jit(solution)/shard_map/look_back/pallas_call | solution.py:314
  337.2 10.9 %read_back.1 = (f32[512,768]{1,0:T(8,128)}, bf16[512,768]{1,0:T(8,128)(2,1)}, bf16[512,384]{1,0:T(8,128)(2,1)}, bf16[432,768]{1,0:T(8,128)(2,1)}) custom-call(s32[4]{0:T(128)} %pad_add_fusion.refs_0_, bf16[256,768]{1,0:T(8,128)(2,1)} %refs_1_.7, bf16[256,768]{1,0:T(8,128)(2,1)} %copy-done.5, bf16[512,768]{1,0:T(8,128)(2,1)} %get-tuple-element.77.refs_3_, ...), custom_call_target="tpu_custom_call" | custom-call | flops 6000000000 | bytes 10137616 | tf_op jit(solution)/shard_map/read_back/pallas_call | solution.py:314
  348.0 8.2 %middle_weights.1 = bf16[768,3072]{1,0:T(8,128)(2,1)} custom-call(bf16[432,768]{1,0:T(8,128)(2,1)} %get-tuple-element.105.nv, bf16[512,768]{1,0:T(8,128)(2,1)} %get-tuple-element.106.nq, bf16[432,384]{1,0:T(8,128)(2,1)} %get-tuple-element.76.dq.dq3, bf16[432,768]{1,0:T(8,128)(2,1)} %get-tuple-element.79.dkv.dkv2, bf16[512,384]{1,0:T(8,128)(2,1)} %get-tuple-element.86.dq.dq2, ...), custom_call_target="tpu_custom_call" | custom-call | flops 2500000000 | bytes 10518528 | tf_op jit(solution)/shard_map/middle_weights/pallas_call | solution.py:314
  367.2 11.5 %collective-permute-done.13.refs_3_ = bf16[432,768]{1,0:T(8,128)(2,1)S(1)} collective-permute-done((bf16[432,768]{1,0:T(8,128)(2,1)}, bf16[432,768]{1,0:T(8,128)(2,1)S(1)}, u32[]{:S(2)}, u32[]{:S(2)}) %collective-permute-start.13) | collective-permute-done | bytes 663584 | tf_op jit(solution)/shard_map/ppermute | solution.py:341
  379.6 12.1 %first_back_0.1 = (f32[216,768]{1,0:T(8,128)}, bf16[432,768]{1,0:T(8,128)(2,1)}, bf16[432,1152]{1,0:T(8,128)(2,1)}, bf16[216,768]{1,0:T(8,128)(2,1)}, f32[216,768]{1,0:T(8,128)}, /*index=5*/f32[1,768]{1,0:T(1,128)}) custom-call(s32[4]{0:T(128)} %pad_add_fusion.refs_0_, f32[432,768]{1,0:T(8,128)} %get-tuple-element.75.refs_1_, ...), custom_call_target="tpu_custom_call" | custom-call | flops 7000000000 | bytes 12008464 | tf_op jit(solution)/shard_map/first_back_0/pallas_call | solution.py:314
  394.0 14.3 %first_back_1.1 = (f32[256,768]{1,0:T(8,128)}, bf16[512,768]{1,0:T(8,128)(2,1)}, bf16[512,1152]{1,0:T(8,128)(2,1)}, bf16[256,768]{1,0:T(8,128)(2,1)}, f32[256,768]{1,0:T(8,128)}, /*index=5*/f32[1,768]{1,0:T(1,128)}) custom-call(s32[4]{0:T(128)} %pad_add_fusion.refs_0_, f32[512,768]{1,0:T(8,128)} %get-tuple-element.85.refs_1_, ...), custom_call_target="tpu_custom_call" | custom-call | flops 7000000000 | bytes 13794320 | tf_op jit(solution)/shard_map/first_back_1/pallas_call | solution.py:314
  408.2 8.0 %first_weights.1 = bf16[768,3200]{1,0:T(8,128)(2,1)} custom-call(bf16[432,768]{1,0:T(8,128)(2,1)} %get-tuple-element.93.n0, bf16[512,768]{1,0:T(8,128)(2,1)} %get-tuple-element.94.n1, bf16[432,1152]{1,0:T(8,128)(2,1)} %get-tuple-element.95.d0, bf16[512,1152]{1,0:T(8,128)(2,1)} %get-tuple-element.96.d1, bf16[432,768]{1,0:T(8,128)(2,1)} %get-tuple-element.97.dy0, ...), custom_call_target="tpu_custom_call" | custom-call | flops 3000000000 | bytes 10733568 | tf_op jit(solution)/shard_map/first_weights/pallas_call | solution.py:314
  421.3 6.7 %collective-permute-done.7 = bf16[216,768]{1,0:T(8,128)(2,1)S(1)} collective-permute-done((bf16[216,768]{1,0:T(8,128)(2,1)S(1)}, bf16[216,768]{1,0:T(8,128)(2,1)S(1)}, u32[]{:S(2)}, u32[]{:S(2)}) %collective-permute-start.7) | collective-permute-done | bytes 331808 | tf_op jit(solution)/shard_map/ppermute | solution.py:341
  428.7 7.6 %collective-permute-done.10 = bf16[256,768]{1,0:T(8,128)(2,1)S(1)} collective-permute-done((bf16[256,768]{1,0:T(8,128)(2,1)S(1)}, bf16[256,768]{1,0:T(8,128)(2,1)S(1)}, u32[]{:S(2)}, u32[]{:S(2)}) %collective-permute-start.10) | collective-permute-done | bytes 393248 | tf_op jit(solution)/shard_map/ppermute | solution.py:341
  437.2 6.3 %collective-permute-done.14.refs_2_ = bf16[216,768]{1,0:T(8,128)(2,1)S(1)} collective-permute-done((bf16[216,768]{1,0:T(8,128)(2,1)S(1)}, bf16[216,768]{1,0:T(8,128)(2,1)S(1)}, u32[]{:S(2)}, u32[]{:S(2)}) %collective-permute-start.14) | collective-permute-done | bytes 331808 | tf_op jit(solution)/shard_map/ppermute | solution.py:341
  461.2 33.8 %reduce-scatter.7.cloned.1.call-done = bf16[48,3072]{1,0:T(8,128)(2,1)} async-done(((bf16[768,3072]{1,0:T(8,128)(2,1)}), bf16[48,3072]{1,0:T(8,128)(2,1)}) %reduce-scatter.7.cloned.1.call-update) | async-done | bytes 294928 | tf_op jit(solution)/shard_map/reduce_scatter | solution.py:347
  497.5 78.5 %reduce-scatter.5.cloned.1.call-done = bf16[48,3200]{1,0:T(8,128)(2,1)} async-done(((bf16[768,3200]{1,0:T(8,128)(2,1)}), bf16[48,3200]{1,0:T(8,128)(2,1)}) %reduce-scatter.5.cloned.1.call-update) | async-done | bytes 307216 | tf_op jit(solution)/shard_map/reduce_scatter | solution.py:347
  (171 shorter events, 108.7 us)
Async XLA Ops:
  7.2 54.2 %all-gather.5.cloned.1.call-start = ((), (), s32[]{:S(2)}) async-start(), calls=%async_computation.4 | async-start | bytes 3969024 | tf_op jit(solution)/shard_map/all_gather | solution.py:344
  10.2 100.2 %all-gather.9.cloned.1.call-start = ((), (), s32[]{:S(2)}) async-start(), calls=%async_computation.6 | async-start | bytes 3760128 | tf_op jit(solution)/shard_map/all_gather | solution.py:344
  11.1 154.6 %all-gather.7.cloned.1.call-start = ((), (), s32[]{:S(2)}) async-start(), calls=%async_computation.5 | async-start | bytes 5013504 | tf_op jit(solution)/shard_map/all_gather | solution.py:344
  18.8 229.7 %all-gather.11.cloned.1.call-start = ((), (), s32[]{:S(2)}) async-start(), calls=%async_computation.7 | async-start | bytes 10027008 | tf_op jit(solution)/shard_map/all_gather | solution.py:344
  19.9 432.3 %reduce-scatter.9.cloned.1.call-start = ((), (), s32[]{:S(2)}) async-start(), calls=%async_computation.10 | async-start | bytes 5013504 | tf_op jit(solution)/shard_map/reduce_scatter | solution.py:347
  20.0 10.8 %collective-permute-start = (bf16[216,768]{1,0:T(8,128)(2,1)S(1)}, bf16[216,768]{1,0:T(8,128)(2,1)S(1)}, u32[]{:S(2)}, u32[]{:S(2)}) collective-permute-start(bf16[216,768]{1,0:T(8,128)(2,1)S(1)} %copy-done.14), channel_id=1, source_target_pairs={{0,1},{1,0},{2,3},{3,2},{4,5},{5,4},{6,7},{7,6},{8,9},{9,8},{10,11... | collective-permute-start | bytes 995336 | tf_op jit(solution)/shard_map/ppermute | solution.py:341
  21.8 46.8 %collective-permute-start.3 = (bf16[256,768]{1,0:T(8,128)(2,1)S(1)}, bf16[256,768]{1,0:T(8,128)(2,1)S(1)}, u32[]{:S(2)}, u32[]{:S(2)}) collective-permute-start(bf16[256,768]{1,0:T(8,128)(2,1)S(1)} %copy-done.7), channel_id=1, source_target_pairs={{0,1},{1,0},{2,3},{3,2},{4,5},{5,4},{6,7},{7,6},{8,9},{9,8},{10,11... | collective-permute-start | bytes 1179656 | tf_op jit(solution)/shard_map/ppermute | solution.py:341
  67.1 43.3 %collective-permute-start.1 = (bf16[432,384]{1,0:T(8,128)(2,1)}, bf16[432,384]{1,0:T(8,128)(2,1)S(1)}, u32[]{:S(2)}, u32[]{:S(2)}) collective-permute-start(bf16[432,384]{1,0:T(8,128)(2,1)} %get-tuple-element.61.refs_1_.o0), channel_id=1, source_target_pairs={{0,1},{1,0},{2,3},{3,2},{4,5},{5,4},{6,7},{7,6},{8,9},{9,8},{10,11... | collective-permute-start | bytes 995336 | tf_op jit(solution)/shard_map/ppermute | solution.py:341
  75.9 95.7 %collective-permute-start.4 = (bf16[512,384]{1,0:T(8,128)(2,1)}, bf16[512,384]{1,0:T(8,128)(2,1)S(1)}, u32[]{:S(2)}, u32[]{:S(2)}) collective-permute-start(bf16[512,384]{1,0:T(8,128)(2,1)} %get-tuple-element.66.refs_1_.o1), channel_id=1, source_target_pairs={{0,1},{1,0},{2,3},{3,2},{4,5},{5,4},{6,7},{7,6},{8,9},{9,8},{10,11... | collective-permute-start | bytes 1179656 | tf_op jit(solution)/shard_map/ppermute | solution.py:341
  76.3 108.6 %collective-permute-start.6 = (bf16[216,768]{1,0:T(8,128)(2,1)S(1)}, bf16[216,768]{1,0:T(8,128)(2,1)S(1)}, u32[]{:S(2)}, u32[]{:S(2)}) collective-permute-start(bf16[216,768]{1,0:T(8,128)(2,1)S(1)} %copy-done.10), channel_id=1, source_target_pairs={{0,1},{1,0},{2,3},{3,2},{4,5},{5,4},{6,7},{7,6},{8,9},{9,8},{10,11... | collective-permute-start | bytes 995336 | tf_op jit(solution)/shard_map/ppermute | solution.py:341
  183.5 10.2 %collective-permute-start.5 = (bf16[432,384]{1,0:T(8,128)(2,1)}, bf16[432,384]{1,0:T(8,128)(2,1)S(1)}, u32[]{:S(2)}, u32[]{:S(2)}) collective-permute-start(bf16[432,384]{1,0:T(8,128)(2,1)} %look.1.refs_2_.o_look), channel_id=1, source_target_pairs={{0,1},{1,0},{2,3},{3,2},{4,5},{5,4},{6,7},{7,6},{8,9},{9,8},{10,11... | collective-permute-start | bytes 995336 | tf_op jit(solution)/shard_map/ppermute | solution.py:341
  263.9 189.6 %reduce-scatter.11.cloned.1.call-start = ((), (), s32[]{:S(2)}) async-start(), calls=%async_computation.11 | async-start | bytes 5013504 | tf_op jit(solution)/shard_map/reduce_scatter | solution.py:347
  264.8 11.9 %collective-permute-start.9 = (bf16[256,768]{1,0:T(8,128)(2,1)S(1)}, bf16[256,768]{1,0:T(8,128)(2,1)S(1)}, u32[]{:S(2)}, u32[]{:S(2)}) collective-permute-start(bf16[256,768]{1,0:T(8,128)(2,1)S(1)} %copy-done.4), channel_id=1, source_target_pairs={{0,1},{1,0},{2,3},{3,2},{4,5},{5,4},{6,7},{7,6},{8,9},{9,8},{10,11... | collective-permute-start | bytes 1179656 | tf_op jit(solution)/shard_map/ppermute | solution.py:341
  271.1 13.4 %collective-permute-start.8 = (bf16[512,384]{1,0:T(8,128)(2,1)}, bf16[512,384]{1,0:T(8,128)(2,1)S(1)}, u32[]{:S(2)}, u32[]{:S(2)}) collective-permute-start(bf16[512,384]{1,0:T(8,128)(2,1)} %read.1.refs_2_.o_read), channel_id=1, source_target_pairs={{0,1},{1,0},{2,3},{3,2},{4,5},{5,4},{6,7},{7,6},{8,9},{9,8},{10,11... | collective-permute-start | bytes 1179656 | tf_op jit(solution)/shard_map/ppermute | solution.py:341
  302.1 192.8 %reduce-scatter.7.cloned.1.call-start = ((), (), s32[]{:S(2)}) async-start(), calls=%async_computation.9 | async-start | bytes 5013504 | tf_op jit(solution)/shard_map/reduce_scatter | solution.py:347
  303.2 17.8 %collective-permute-start.11 = (bf16[432,768]{1,0:T(8,128)(2,1)S(1)}, bf16[432,768]{1,0:T(8,128)(2,1)S(1)}, u32[]{:S(2)}, u32[]{:S(2)}) collective-permute-start(bf16[432,768]{1,0:T(8,128)(2,1)S(1)} %copy-done.23), channel_id=1, source_target_pairs={{0,1},{1,0},{2,3},{3,2},{4,5},{5,4},{6,7},{7,6},{8,9},{9,8},{10,11... | collective-permute-start | bytes 1990664 | tf_op jit(solution)/shard_map/ppermute | solution.py:341
  304.7 31.6 %collective-permute-start.12 = (bf16[512,768]{1,0:T(8,128)(2,1)S(1)}, bf16[512,768]{1,0:T(8,128)(2,1)S(1)}, u32[]{:S(2)}, u32[]{:S(2)}) collective-permute-start(bf16[512,768]{1,0:T(8,128)(2,1)S(1)} %copy-done.20), channel_id=1, source_target_pairs={{0,1},{1,0},{2,3},{3,2},{4,5},{5,4},{6,7},{7,6},{8,9},{9,8},{10,11... | collective-permute-start | bytes 2359304 | tf_op jit(solution)/shard_map/ppermute | solution.py:341
  356.2 219.7 %reduce-scatter.5.cloned.1.call-start = ((), (), s32[]{:S(2)}) async-start(), calls=%async_computation.8 | async-start | bytes 5222400 | tf_op jit(solution)/shard_map/reduce_scatter | solution.py:347
  360.6 18.1 %collective-permute-start.13 = (bf16[432,768]{1,0:T(8,128)(2,1)}, bf16[432,768]{1,0:T(8,128)(2,1)S(1)}, u32[]{:S(2)}, u32[]{:S(2)}) collective-permute-start(bf16[432,768]{1,0:T(8,128)(2,1)} %get-tuple-element.80.refs_2_), channel_id=1, source_target_pairs={{0,1},{1,0},{2,3},{3,2},{4,5},{5,4},{6,7},{7,6},{8,9},{9,8},{10,11... | collective-permute-start | bytes 1990664 | tf_op jit(solution)/shard_map/ppermute | solution.py:341
  366.5 26.5 %collective-permute-start.15 = (bf16[512,768]{1,0:T(8,128)(2,1)}, bf16[512,768]{1,0:T(8,128)(2,1)S(1)}, u32[]{:S(2)}, u32[]{:S(2)}) collective-permute-start(bf16[512,768]{1,0:T(8,128)(2,1)} %get-tuple-element.88.refs_2_), channel_id=1, source_target_pairs={{0,1},{1,0},{2,3},{3,2},{4,5},{5,4},{6,7},{7,6},{8,9},{9,8},{10,11... | collective-permute-start | bytes 2359304 | tf_op jit(solution)/shard_map/ppermute | solution.py:341
  417.2 10.7 %collective-permute-start.7 = (bf16[216,768]{1,0:T(8,128)(2,1)S(1)}, bf16[216,768]{1,0:T(8,128)(2,1)S(1)}, u32[]{:S(2)}, u32[]{:S(2)}) collective-permute-start(bf16[216,768]{1,0:T(8,128)(2,1)S(1)} %copy-done.29), channel_id=1, source_target_pairs={{0,1},{1,0},{2,3},{3,2},{4,5},{5,4},{6,7},{7,6},{8,9},{9,8},{10,11... | collective-permute-start | bytes 995336 | tf_op jit(solution)/shard_map/ppermute | solution.py:341
  418.6 17.8 %collective-permute-start.10 = (bf16[256,768]{1,0:T(8,128)(2,1)S(1)}, bf16[256,768]{1,0:T(8,128)(2,1)S(1)}, u32[]{:S(2)}, u32[]{:S(2)}) collective-permute-start(bf16[256,768]{1,0:T(8,128)(2,1)S(1)} %copy-done.26), channel_id=1, source_target_pairs={{0,1},{1,0},{2,3},{3,2},{4,5},{5,4},{6,7},{7,6},{8,9},{9,8},{10,11... | collective-permute-start | bytes 1179656 | tf_op jit(solution)/shard_map/ppermute | solution.py:341
  419.2 24.2 %collective-permute-start.14 = (bf16[216,768]{1,0:T(8,128)(2,1)S(1)}, bf16[216,768]{1,0:T(8,128)(2,1)S(1)}, u32[]{:S(2)}, u32[]{:S(2)}) collective-permute-start(bf16[216,768]{1,0:T(8,128)(2,1)S(1)} %copy-done.30), channel_id=1, source_target_pairs={{0,1},{1,0},{2,3},{3,2},{4,5},{5,4},{6,7},{7,6},{8,9},{9,8},{10,11... | collective-permute-start | bytes 995336 | tf_op jit(solution)/shard_map/ppermute | solution.py:341
  420.6 27.9 %collective-permute-start.16 = (bf16[256,768]{1,0:T(8,128)(2,1)S(1)}, bf16[256,768]{1,0:T(8,128)(2,1)S(1)}, u32[]{:S(2)}, u32[]{:S(2)}) collective-permute-start(bf16[256,768]{1,0:T(8,128)(2,1)S(1)} %copy-done.27), channel_id=1, source_target_pairs={{0,1},{1,0},{2,3},{3,2},{4,5},{5,4},{6,7},{7,6},{8,9},{9,8},{10,11... | collective-permute-start | bytes 1179656 | tf_op jit(solution)/shard_map/ppermute | solution.py:341
  (34 other events, 318.6 us)
Sparse Core Ops, SparseCore 0:
  10.8 50.5 all-gather.4
  64.2 46.2 all-gather.8
  113.3 52.3 all-gather.6
  168.4 79.9 all-gather.10
  264.0 73.6 reduce-scatter.8
  341.9 74.5 reduce-scatter.10
  420.4 74.5 reduce-scatter.6
  499.5 76.4 reduce-scatter.4
